TPU v7x, 32 devices: a whole 2x2x4 slice. The times are simulated.
32 devices in a mesh: fsdp: 4 (over y, x), seq: 8 (over z, core).
Axes of the slice: x: 2, y: 2, z: 4, core: 2. Of those that a mesh axis runs over, the one named last changes fastest.
Arguments:
- hidden: bfloat16 [4, 1024, 5120], P('fsdp', 'seq'), may hold values from -6 to 6
- queries: bfloat16 [4, 1024, 4096], P('fsdp', 'seq'), may hold values from -400 to 400
- key_value_weight: bfloat16 [5120, 2048], P('fsdp'), may hold values from -0.078125 to 0.078125
- doc_lengths: int32 [4, 8], P('fsdp'), may hold values from 1 to 512, 1024 in all within a row
- resp_lengths: int32 [4, 8], P('fsdp'), may hold values from 1 to 128
Outputs:
- attended: bfloat16 [4, 1024, 4096], P('fsdp', 'seq')
- pooled: float32 [4, 8, 4096], P('fsdp', None, 'seq')
Inputs may be any that keep to these rules, and one draw needn't show every extreme that they name: `doc_lengths`: each row holds the lengths of the documents of one packed sequence in order; they sum to 1024 and the longest is exactly 512.
All inputs are finite; a program needn't handle non-finite values.
Results may differ from a plain program's by a relative error of at most 0.011.
Values may be sent and summed in bfloat16 or wider, within the bound.
A program may use at most 128 MiB of HBM per device.

v0:
```python
import jax
import jax.numpy as jnp
from jax import lax
from jax.sharding import PartitionSpec as P

HEAD_SIZE = 128
KEY_VALUE_HEADS = 8


ROPE_BASE = 1000000.0


def token_tables(lengths, wanted, first, count):
    ends = jnp.cumsum(lengths)
    starts = ends - lengths
    answer = jnp.minimum(wanted, lengths)
    index = first + jnp.arange(count, dtype=jnp.int32)
    inside = (index[:, None] >= starts[None, :]) & (index[:, None] < ends[None, :])
    token_position = jnp.sum(jnp.where(inside, index[:, None] - starts[None, :], 0), axis=1)
    doc_id = jnp.sum(jnp.where(index[:, None] >= ends[None, :], 1, 0), axis=1).astype(jnp.int32)
    member = jnp.where(inside & (index[:, None] >= (ends - answer)[None, :]), 1, 0).astype(
        jnp.int32
    )
    return (token_position, doc_id, member, answer)


def rotate_pairs(heads, token_position):
    half = heads.shape[-1] // 2
    freq = ROPE_BASE ** (-(jnp.arange(half, dtype=jnp.float32) * 2.0 / heads.shape[-1]))
    angle = token_position.astype(jnp.float32)[:, None] * freq[None, :]
    cosine = jnp.cos(angle)[:, None, :]
    sine = jnp.sin(angle)[:, None, :]
    first = heads[..., :half]
    second = heads[..., half:]
    return jnp.concatenate(
        [first * cosine - second * sine, second * cosine + first * sine], axis=-1
    )


def on_device(hidden, queries, key_value_weight, doc_lengths, resp_lengths):
    piece_list = lax.axis_size("seq")
    rank = lax.axis_index("seq")
    token_batch = hidden.shape[1]
    length = token_batch * piece_list
    longest = length // 2
    kv_cols = key_value_weight.shape[1]
    key_value_split = kv_cols // 2
    lengths = doc_lengths[0]
    wanted = resp_lengths[0]
    spread = lax.all_to_all(hidden, "fsdp", split_axis=2, concat_axis=0, tiled=True)
    projected_rows = lax.psum_scatter(
        jnp.einsum("btd,dc->btc", spread, key_value_weight, preferred_element_type=jnp.float32),
        "fsdp",
        scatter_dimension=0,
        tiled=True,
    )[0]
    local_tables = token_tables(lengths, wanted, rank * token_batch, token_batch)
    key_rows = rotate_pairs(
        projected_rows[:, :key_value_split].reshape(token_batch, KEY_VALUE_HEADS, HEAD_SIZE),
        local_tables[0],
    ).astype(jnp.bfloat16)
    value_rows = (
        projected_rows[:, key_value_split:]
        .reshape(token_batch, KEY_VALUE_HEADS, HEAD_SIZE)
        .astype(jnp.bfloat16)
    )
    repeat_heads = max(1, piece_list // KEY_VALUE_HEADS)
    key_rows = jnp.broadcast_to(
        key_rows[:, :, None, :], (token_batch, KEY_VALUE_HEADS, repeat_heads, HEAD_SIZE)
    ).reshape(1, token_batch, KEY_VALUE_HEADS * repeat_heads * HEAD_SIZE)
    value_rows = jnp.broadcast_to(
        value_rows[:, :, None, :], (token_batch, KEY_VALUE_HEADS, repeat_heads, HEAD_SIZE)
    ).reshape(1, token_batch, KEY_VALUE_HEADS * repeat_heads * HEAD_SIZE)
    q_heads, k_heads, v_heads = (
        lax.all_to_all(queries, "seq", split_axis=2, concat_axis=1, tiled=True),
        lax.all_to_all(key_rows, "seq", split_axis=2, concat_axis=1, tiled=True),
        lax.all_to_all(value_rows, "seq", split_axis=2, concat_axis=1, tiled=True),
    )
    q_count = q_heads.shape[2] // HEAD_SIZE
    kv_count = k_heads.shape[2] // HEAD_SIZE
    query_group = q_count // kv_count
    all_tables = token_tables(lengths, wanted, jnp.int32(0), length)
    doc_id = all_tables[1]
    answer = all_tables[3]
    query_matrix = q_heads[0].reshape(length, kv_count, query_group, HEAD_SIZE)
    key_all = k_heads[0].reshape(length, kv_count, HEAD_SIZE)
    value_all = v_heads[0].reshape(length, kv_count, HEAD_SIZE)
    block = min(512, length)
    window = min(length, block + longest)

    def attend(index):
        qstart = index * block
        kstart = jnp.maximum(qstart + block - window, 0)
        qblock = lax.dynamic_slice_in_dim(query_matrix, qstart, block, 0)
        kblock = lax.dynamic_slice_in_dim(key_all, kstart, window, 0)
        vblock = lax.dynamic_slice_in_dim(value_all, kstart, window, 0)
        qdoc = lax.dynamic_slice_in_dim(doc_id, qstart, block, 0)
        kdoc = lax.dynamic_slice_in_dim(doc_id, kstart, window, 0)
        qplace = qstart + jnp.arange(block, dtype=jnp.int32)
        kplace = kstart + jnp.arange(window, dtype=jnp.int32)
        allowed = (qdoc[:, None] == kdoc[None, :]) & (kplace[None, :] <= qplace[:, None])
        scores = jnp.einsum(
            "qkgd,skd->kgqs", qblock, kblock, preferred_element_type=jnp.float32
        ) * HEAD_SIZE ** (-0.5)
        scores = jnp.where(allowed, scores, -1e30)
        peak = jnp.max(scores, axis=-1, keepdims=True)
        weight = jnp.where(allowed, jnp.exp(scores - peak), 0.0)
        probs = (weight / jnp.sum(weight, axis=-1, keepdims=True)).astype(jnp.bfloat16)
        output = jnp.einsum("kgqs,skd->qkgd", probs, vblock, preferred_element_type=jnp.float32)
        return output.astype(jnp.bfloat16).reshape(block, q_count * HEAD_SIZE)

    attn_heads = lax.map(attend, jnp.arange(length // block, dtype=jnp.int32)).reshape(
        length, q_count * HEAD_SIZE
    )
    attended = lax.all_to_all(attn_heads[None], "seq", split_axis=1, concat_axis=2, tiled=True)
    partial_value = jnp.einsum(
        "tr,tc->rc",
        local_tables[2].astype(jnp.bfloat16),
        attended[0],
        preferred_element_type=jnp.float32,
    )
    sums = lax.psum_scatter(
        partial_value.astype(jnp.bfloat16), "seq", scatter_dimension=1, tiled=True
    ).astype(jnp.float32)
    pooled = sums / answer.astype(jnp.float32)[:, None]
    return (attended, pooled[None])


def solution(mesh):
    in_specs = (
        P("fsdp", "seq", None),
        P("fsdp", "seq", None),
        P("fsdp", None),
        P("fsdp", None),
        P("fsdp", None),
    )
    out_specs = (P("fsdp", "seq", None), P("fsdp", None, "seq"))
    return jax.shard_map(
        on_device, mesh=mesh, in_specs=in_specs, out_specs=out_specs, check_vma=False
    )
```

profile of v0, /device:TPU:25, one launch (start us, length us, event | category | flops | bytes accessed | tf_op | source)
XLA Modules:
  0.0 262.3 jit_solution(8647189720159909940)
XLA Ops:
  7.2 4.8 %copy.72 = bf16[1,128,5120]{1,0,2:T(2,128)(2,1)S(1)} copy(bf16[1,128,5120]{2,1,0:T(8,128)(2,1)} %param.7) | data formatting | bytes 2621440 | tf_op args[0]
  12.0 0.5 broadcast.95
  12.6 28.9 %reduce.15 = bf16[5120,128]{1,0:T(8,128)(2,1)} reduce(bf16[5120,1,128]{2,1,0:T(2,128)(2,1)S(1)} %bitcast.135, bf16[]{:T(256)} %broadcast.95), dimensions={1}, to_apply=%bitcast.99.reduce_sub_computation | reduce | bytes 2621442
  41.4 2.3 reshape.194
  43.7 19.0 %all_to_all.81 = bf16[4,2,81920]{2,1,0:T(2,128)(2,1)} all-to-all(bf16[4,2,81920]{2,1,0:T(2,128)(2,1)S(1)} %reshape.194), channel_id=1, replica_groups=mesh['fsdp'=4,'seq'=8] {'fsdp'}, dimensions={0} | all-to-all | bytes 2621440 | tf_op jit(solution)/shard_map/all_to_all | solution.py:50
  62.7 2.8 %reshape.195 = bf16[5120,1,128]{2,1,0:T(2,128)(2,1)S(1)} reshape(bf16[4,2,81920]{2,1,0:T(2,128)(2,1)} %all_to_all.81) | data formatting | bytes 2621440
  65.6 1.2 copy.90
  66.8 1.6 copy.73
  68.4 7.0 %fusion.16 = f32[4,128,2048]{2,1,0:T(8,128)} fusion(bf16[1280,2048]{1,0:T(8,128)(2,1)} %param.9, bf16[1,128,4,1280]{3,1,2,0:T(8,128)(2,1)S(1)} %copy.73), kind=kOutput, calls=%fused_computation.21 | convolution fusion | flops 2684354560 | bytes 10747904 | tf_op jit(solution)/shard_map/btd,dc->btc/dot_general | solution.py:52
  75.5 2.8 %copy.70 = bf16[1,128,4096]{1,0,2:T(2,128)(2,1)S(1)} copy(bf16[1,128,4096]{2,1,0:T(8,128)(2,1)S(1)} %copy-done) | data formatting | bytes 2097152 | tf_op args[1]
  78.3 22.4 %reduce.14 = bf16[4096,128]{1,0:T(8,128)(2,1)S(1)} reduce(bf16[4096,1,128]{2,1,0:T(2,128)(2,1)S(1)} %bitcast.143, bf16[]{:T(256)} %broadcast.95), dimensions={1}, to_apply=%bitcast.97.reduce_sub_computation | reduce | bytes 2097154
  100.7 1.1 reshape.192
  101.8 7.0 %all-to-all-start = ((bf16[8,2,32768]{2,1,0:T(2,128)(2,1)}), bf16[8,2,32768]{2,1,0:T(2,128)(2,1)S(1)}, u32[]{:S(2)}, u32[]{:S(2)}) async-start(bf16[8,2,32768]{2,1,0:T(2,128)(2,1)} %reshape.192), calls=%async_computation | async-start | bytes 2097152 | tf_op jit(solution)/shard_map/all_to_all | solution.py:75
  108.8 0.2 reduce-window.4
  109.0 0.1 select_reduce_fusion.1
  109.1 0.2 multiply_cosine_fusion
  109.3 20.0 %reduce-scatter.7.cloned.1.call-done = f32[1,128,2048]{2,1,0:T(8,128)} async-done(((f32[4,128,2048]{2,1,0:T(8,128)}), f32[1,128,2048]{2,1,0:T(8,128)}) %reduce-scatter.7.cloned.1.call-update) | async-done | bytes 1048592
  129.3 1.1 slice.17
  130.4 0.2 copy.74
  130.7 0.4 copy.97
  131.1 2.2 reduce.16
  133.3 0.8 reshape.196
  134.1 5.4 %all-to-all-start.2 = ((bf16[8,2,8192]{2,1,0:T(2,128)(2,1)}), bf16[8,2,8192]{2,1,0:T(2,128)(2,1)S(1)}, u32[]{:S(2)}, u32[]{:S(2)}) async-start(bf16[8,2,8192]{2,1,0:T(2,128)(2,1)} %reshape.196), calls=%async_computation.2 | async-start | bytes 524288 | tf_op jit(solution)/shard_map/all_to_all | solution.py:76
  139.5 1.1 fusion.19
  140.6 0.4 copy.77
  141.0 2.2 reduce.17
  143.2 0.8 reshape.198
  143.9 2.7 %all-to-all-done.2 = bf16[8,2,8192]{2,1,0:T(2,128)(2,1)S(1)} async-done(((bf16[8,2,8192]{2,1,0:T(2,128)(2,1)}), bf16[8,2,8192]{2,1,0:T(2,128)(2,1)S(1)}, u32[]{:S(2)}, u32[]{:S(2)}) %all-to-all-start.2) | async-done | bytes 262176 | tf_op jit(solution)/shard_map/all_to_all | solution.py:76
  146.6 6.6 %all-to-all-start.3 = ((bf16[8,2,8192]{2,1,0:T(2,128)(2,1)}), bf16[8,2,8192]{2,1,0:T(2,128)(2,1)}, u32[]{:S(2)}, u32[]{:S(2)}) async-start(bf16[8,2,8192]{2,1,0:T(2,128)(2,1)} %reshape.198), calls=%async_computation.3 | async-start | bytes 524288 | tf_op jit(solution)/shard_map/all_to_all | solution.py:77
  153.2 0.1 select_reduce_fusion
  153.3 1.1 reshape.193
  154.3 0.1 copy.89
  154.5 0.7 copy.71
  155.2 0.5 reshape_squeeze.9
  155.7 1.2 reshape.197
  156.9 0.2 copy.76
  157.1 3.3 %all-to-all-done.3 = bf16[8,2,8192]{2,1,0:T(2,128)(2,1)} async-done(((bf16[8,2,8192]{2,1,0:T(2,128)(2,1)}), bf16[8,2,8192]{2,1,0:T(2,128)(2,1)}, u32[]{:S(2)}, u32[]{:S(2)}) %all-to-all-start.3) | async-done | bytes 262176 | tf_op jit(solution)/shard_map/all_to_all | solution.py:77
  160.3 1.2 reshape.199
  161.6 0.2 copy.78
  161.8 0.8 copy.80
  162.6 22.6 %while.14 = (s32[]{:T(128)}, bf16[2,512,512]{2,1,0:T(8,128)(2,1)S(1)}, s32[2]{0:T(128)S(1)}, s32[1024]{0:T(1024)S(1)}, bf16[1024,1,4,128]{0,3,2,1:T(8,128)(2,1)S...) while((s32[]{:T(128)}, ...), condition=%wide.region_7.8_spmd, body=%wide.region_4.7_spmd.sunk | while | flops 1104934400 | bytes 30996700 | solution.py:112
  162.6 0.6 dynamic_slice.41
  163.9 0.5 compare_and_fusion.3
  164.4 1.9 fusion.38
  166.3 3.0 %fusion.39 = f32[4,512]{1,0:T(4,128)S(1)} fusion(f32[512,4,1024]{2,0,1:T(8,128)S(1)} %get-tuple-element.264, f32[4,512]{1,0:T(4,128)S(1)} %get-tuple-element.265, pred[512,1024]{1,0:T(8,128)(4,1)S(1)} %compare_and_fusion.3), kind=kLoop, calls=%fused_computation.4.clone.1 | loop fusion | flops 10483712 | bytes 8929280 | tf_op jit(solution)/shard_map/while/body/eval_jaxpr/reduce_sum | solution.py:108
  169.3 4.2 %fusion.40 = bf16[4,512,128]{1,2,0:T(8,128)(2,1)S(1)} fusion(f32[4,512]{1,0:T(4,128)S(1)} %fusion.39, f32[4,512]{1,0:T(4,128)S(1)} %get-tuple-element.265, f32[512,4,1024]{2,0,1:T(8,128)S(1)} %get-tuple-element.264, pred[512,1024]{1,0:T(8,128)(4,1)S(1)} %compare_and_fusion.3, bf16[1024,1,128]{0,2,1:T(8,128)(2,1)} %get-tuple-element.296), kind=kOutput, calls=%fused_computation.8.clone.1 | convolution fusion | flops 549715968 | bytes 9715712 | tf_op jit(solution)/shard_map/while/body/eval_jaxpr/kgqs,skd->qkgd/dot_general | solution.py:109
  173.5 0.2 copy.99
  173.8 0.6 dynamic_slice.41
  175.1 0.5 compare_and_fusion.3
  175.6 1.9 fusion.38
  177.5 3.0 %fusion.39 = f32[4,512]{1,0:T(4,128)S(1)} fusion(f32[512,4,1024]{2,0,1:T(8,128)S(1)} %get-tuple-element.264, f32[4,512]{1,0:T(4,128)S(1)} %get-tuple-element.265, pred[512,1024]{1,0:T(8,128)(4,1)S(1)} %compare_and_fusion.3), kind=kLoop, calls=%fused_computation.4.clone.1 | loop fusion | flops 10483712 | bytes 8929280 | tf_op jit(solution)/shard_map/while/body/eval_jaxpr/reduce_sum | solution.py:108
  180.5 4.2 %fusion.40 = bf16[4,512,128]{1,2,0:T(8,128)(2,1)S(1)} fusion(f32[4,512]{1,0:T(4,128)S(1)} %fusion.39, f32[4,512]{1,0:T(4,128)S(1)} %get-tuple-element.265, f32[512,4,1024]{2,0,1:T(8,128)S(1)} %get-tuple-element.264, pred[512,1024]{1,0:T(8,128)(4,1)S(1)} %compare_and_fusion.3, bf16[1024,1,128]{0,2,1:T(8,128)(2,1)} %get-tuple-element.296), kind=kOutput, calls=%fused_computation.8.clone.1 | convolution fusion | flops 549715968 | bytes 9715712 | tf_op jit(solution)/shard_map/while/body/eval_jaxpr/kgqs,skd->qkgd/dot_general | solution.py:109
  184.7 0.2 copy.99
  185.2 1.6 copy.96
  186.8 7.0 %reduce.18 = bf16[1024,512]{1,0:T(8,128)(2,1)S(1)} reduce(bf16[1024,1,512]{2,1,0:T(2,128)(2,1)S(1)} %bitcast.142, bf16[]{:T(256)} %broadcast.95), dimensions={1}, to_apply=%bitcast.114.reduce_sub_computation | reduce | bytes 2097154
  193.9 0.8 reshape.200
  194.7 29.0 %all_to_all.82 = bf16[8,2,32768]{2,1,0:T(2,128)(2,1)S(1)} all-to-all(bf16[8,2,32768]{2,1,0:T(2,128)(2,1)S(1)} %reshape.200), channel_id=1, replica_groups=mesh['fsdp'=4,'seq'=8] {'seq'}, dimensions={0} | all-to-all | bytes 2097152 | tf_op jit(solution)/shard_map/all_to_all | solution.py:115
  223.7 1.0 reshape.201
  224.8 0.3 copy.93
  225.0 0.7 copy.83
  225.7 1.0 convolution_convert_fusion
  226.8 1.3 copy.85
  228.1 26.0 %reduce-scatter.5.cloned.1.call-done = bf16[8,512]{1,0:T(8,128)(2,1)} async-done(((bf16[8,4096]{1,0:T(8,128)(2,1)}), bf16[8,512]{1,0:T(8,128)(2,1)}) %reduce-scatter.5.cloned.1.call-update) | async-done | bytes 8208 | tf_op jit(solution)/shard_map/reduce_scatter | solution.py:122
  254.1 1.4 divide_bitcast_fusion
  (33 shorter events, 0.5 us)
Async XLA Ops:
  7.2 122.1 %reduce-scatter.7.cloned.1.call-start = ((), (), s32[]{:S(2)}) async-start(), calls=%async_computation.8 | async-start | bytes 5242880
  68.4 7.0 %copy-start = (bf16[1,128,4096]{2,1,0:T(8,128)(2,1)S(1)}, bf16[1,128,4096]{2,1,0:T(8,128)(2,1)}, u32[]{:S(2)}) copy-start(bf16[1,128,4096]{2,1,0:T(8,128)(2,1)} %param.8) | copy-start | bytes 3145732
  75.5 33.3 %copy-start.3 = (s32[1,8]{1,0:T(1,128)S(1)}, s32[1,8]{1,0:T(1,128)}, u32[]{:S(2)}) copy-start(s32[1,8]{1,0:T(1,128)} %param.10) | copy-start | bytes 100
  75.5 33.5 %copy-start.4 = (s32[1,8]{1,0:T(1,128)S(1)}, s32[1,8]{1,0:T(1,128)}, u32[]{:S(2)}) copy-start(s32[1,8]{1,0:T(1,128)} %param.11) | copy-start | bytes 100
  101.8 32.3 %all-to-all-start = ((bf16[8,2,32768]{2,1,0:T(2,128)(2,1)}), bf16[8,2,32768]{2,1,0:T(2,128)(2,1)S(1)}, u32[]{:S(2)}, u32[]{:S(2)}) async-start(bf16[8,2,32768]{2,1,0:T(2,128)(2,1)} %reshape.192), calls=%async_computation | async-start | bytes 2097152 | tf_op jit(solution)/shard_map/all_to_all | solution.py:75
  134.1 12.5 %all-to-all-start.2 = ((bf16[8,2,8192]{2,1,0:T(2,128)(2,1)}), bf16[8,2,8192]{2,1,0:T(2,128)(2,1)S(1)}, u32[]{:S(2)}, u32[]{:S(2)}) async-start(bf16[8,2,8192]{2,1,0:T(2,128)(2,1)} %reshape.196), calls=%async_computation.2 | async-start | bytes 524288 | tf_op jit(solution)/shard_map/all_to_all | solution.py:76
  146.6 6.6 %copy-start.2 = (bf16[8,2,8192]{2,1,0:T(2,128)(2,1)}, bf16[8,2,8192]{2,1,0:T(2,128)(2,1)S(1)}, u32[]{:S(2)}) copy-start(bf16[8,2,8192]{2,1,0:T(2,128)(2,1)S(1)} %all-to-all-done.2) | copy-start | bytes 786436
  146.6 13.8 %all-to-all-start.3 = ((bf16[8,2,8192]{2,1,0:T(2,128)(2,1)}), bf16[8,2,8192]{2,1,0:T(2,128)(2,1)}, u32[]{:S(2)}, u32[]{:S(2)}) async-start(bf16[8,2,8192]{2,1,0:T(2,128)(2,1)} %reshape.198), calls=%async_computation.3 | async-start | bytes 524288 | tf_op jit(solution)/shard_map/all_to_all | solution.py:77
  153.2 100.9 %reduce-scatter.5.cloned.1.call-start = ((), (), s32[]{:S(2)}) async-start(), calls=%async_computation.7 | async-start | bytes 73728 | tf_op jit(solution)/shard_map/reduce_scatter | solution.py:122
  154.5 8.1 %copy-start.1 = (bf16[2,512,512]{2,1,0:T(8,128)(2,1)S(1)}, bf16[2,512,512]{2,1,0:T(8,128)(2,1)}, u32[]{:S(2)}) copy-start(bf16[2,512,512]{2,1,0:T(8,128)(2,1)} %custom-call) | copy-start | bytes 3145732
Sparse Core Ops, SparseCore 0:
  75.6 53.6 reduce-scatter.6
  226.9 27.0 reduce-scatter.4
where the time goes:
time: 268 us; the launch traced here: 262 us
  other arithmetic  71.8 us (27%)
  waiting for transfers between devices  51.9 us (19%)
  blocking collectives  48 us (18%)
  local copies, waits for them, and re-layouts  35.4 us (13%)
  matrix products  20.1 us (8%)
  starting transfers between devices  19 us (7%)
  between operations  14.3 us (5%)
    unnamed x5, other arithmetic  62.7 us
    all_to_all x1, blocking collectives, on_device(): lax.all_to_all(attn_heads[None], 'seq', split_axis=1, concat_axis=2, tile...  29 us
    reduce_scatter x1, waiting for transfers between devices, on_device(): lax.psum_scatter(partial_value.astype(jnp.bfloat16), 'seq', scatter_dimen...  26 us
    unnamed x29, local copies, waits for them, and re-layouts  24.2 us
    unnamed x3, waiting for transfers between devices  20.1 us
    all_to_all x1, blocking collectives, on_device(): lax.all_to_all(hidden, 'fsdp', split_axis=2, concat_axis=0, tiled=True)  19 us
    dot_general x2, matrix products, attend(): jnp.einsum('kgqs,skd->qkgd', probs, vblock, preferred_element_type=jnp.fl...  8.34 us
    dot_general x1, matrix products, on_device(): jnp.einsum('btd,dc->btc', spread, key_value_weight, preferred_element_typ...  6.98 us
  transfers between devices with their start and end apart: 5, of which 4 were waited for; matrix products, arithmetic and copies ran while one was open for 16% of the time, Pallas kernels for 0%

commit v1 on v0

v1 whole, which is shorter than its diff:
```python
import functools
import math

import jax
import jax.numpy as jnp
import numpy as np
from jax import lax
from jax.experimental import pallas as pl
from jax.experimental.pallas import tpu as pltpu
from jax.sharding import PartitionSpec as P

HEAD_SIZE = 128
KEY_VALUE_HEADS = 8
ROPE_BASE = 1000000.0
MASKED = -1e30
MESH = pl.DeviceIdType.MESH


def kernel(
    n,
    ranks,
    hops,
    hidden,
    queries,
    weight,
    lengths,
    wanted,
    freq,
    attended,
    pooled,
    x,
    w,
    q,
    product,
    own,
    outbox,
    inbox,
    kv,
    o,
    bias,
    cosine,
    sine,
    member,
    answers,
    part,
    parts,
    x_sem,
    w_sem,
    q_sem,
    o_sem,
    hid_send,
    hid_recv,
    sum_send,
    sum_recv,
    up_send,
    up_recv,
    pair_send,
    pair_recv,
    pool_send,
    pool_recv,
):
    f = lax.axis_index("fsdp")
    s = lax.axis_index("seq")
    odd = lax.rem(s, 2)
    partner = s + 1 - 2 * odd
    above = lax.rem(s + 2, ranks)
    tokens = x.shape[1]
    depth = x.shape[2]
    half = weight.shape[1] // 2
    q_width = q.shape[2]
    docs = lengths.shape[1]
    blocks = kv.shape[0]
    pool_width = part.shape[2]
    per_head = q_width // pool_width

    def columns(start, size):
        return pl.ds(pl.multiple_of(start, HEAD_SIZE), size)

    def features(j):
        if len(hidden.shape) == 3 and hidden.shape[0] == n and n > 1:
            return hidden.at[j]
        return hidden.at[0, :, columns(j * depth, depth)]

    def w_copy(h, side):
        return pltpu.make_async_copy(
            weight.at[:, columns(side * half + h * HEAD_SIZE, HEAD_SIZE)],
            w.at[h, :, pl.ds(side * HEAD_SIZE, HEAD_SIZE)],
            w_sem.at[h, side],
        )

    def q_copy(h):
        return pltpu.make_async_copy(
            queries.at[0, :, columns(h * q_width, q_width)], q.at[h], q_sem.at[h]
        )

    def o_copy(h):
        return pltpu.make_async_copy(
            o.at[h], attended.at[0, :, columns(h * q_width, q_width)], o_sem.at[h]
        )

    def hid_copy(k):
        j = lax.rem(f + k, n)
        return pltpu.make_async_remote_copy(
            src_ref=features(j),
            dst_ref=x.at[f],
            send_sem=hid_send.at[k],
            recv_sem=hid_recv.at[f],
            device_id=(j, s),
            device_id_type=MESH,
        )

    def hid_arrival(k):
        i = lax.rem(f + k, n)
        return pltpu.make_async_remote_copy(
            src_ref=x.at[i],
            dst_ref=x.at[i],
            send_sem=hid_send.at[k],
            recv_sem=hid_recv.at[i],
            device_id=(i, s),
            device_id_type=MESH,
        )

    def sum_copy(h, k):
        j = lax.rem(f + k, n)
        return pltpu.make_async_remote_copy(
            src_ref=outbox.at[h, j],
            dst_ref=inbox.at[h, f],
            send_sem=sum_send.at[h, k],
            recv_sem=sum_recv.at[h, f],
            device_id=(j, s),
            device_id_type=MESH,
        )

    def sum_arrival(h, k):
        i = lax.rem(f + k, n)
        return pltpu.make_async_remote_copy(
            src_ref=outbox.at[h, i],
            dst_ref=inbox.at[h, i],
            send_sem=sum_send.at[h, k],
            recv_sem=sum_recv.at[h, i],
            device_id=(i, s),
            device_id_type=MESH,
        )

    def up_copy(h, i):
        return pltpu.make_async_remote_copy(
            src_ref=kv.at[2 * i, h],
            dst_ref=kv.at[2 * i + 2, h],
            send_sem=up_send.at[h, i],
            recv_sem=up_recv.at[h, i],
            device_id=(f, above),
            device_id_type=MESH,
        )

    def pair_copy(h, source, m):
        return pltpu.make_async_remote_copy(
            src_ref=kv.at[source, h],
            dst_ref=kv.at[2 * m + 1, h],
            send_sem=pair_send.at[h, m],
            recv_sem=pair_recv.at[h, m],
            device_id=(f, partner),
            device_id_type=MESH,
        )

    def pool_copy(j):
        return pltpu.make_async_remote_copy(
            src_ref=part.at[j],
            dst_ref=parts.at[s],
            send_sem=pool_send.at[j],
            recv_sem=pool_recv.at[s],
            device_id=(f, j),
            device_id_type=MESH,
        )

    def pool_arrival(i):
        return pltpu.make_async_remote_copy(
            src_ref=part.at[i],
            dst_ref=parts.at[i],
            send_sem=pool_send.at[i],
            recv_sem=pool_recv.at[i],
            device_id=(f, i),
            device_id_type=MESH,
        )

    def sends_up(i):
        return (s + 2 < ranks) & (s >= 2 * i)

    def shares_even(m):
        return (odd == 0) & (s >= 2 * m)

    def shares_odd(m):
        return (odd == 1) & (s >= 2 * m + 2)

    own_x = pltpu.make_async_copy(features(f), x.at[f], x_sem)
    own_x.start()

    barrier = pltpu.get_barrier_semaphore()
    for k in range(1, n):
        pl.semaphore_signal(
            barrier, inc=1, device_id=(lax.rem(f + k, n), s), device_id_type=MESH
        )
    for k in range(1, ranks):
        pl.semaphore_signal(
            barrier, inc=1, device_id=(f, lax.rem(s + k, ranks)), device_id_type=MESH
        )
    pl.semaphore_wait(barrier, n + ranks - 2)
    for k in range(1, n):
        hid_copy(k).start()

    @pl.loop(0, KEY_VALUE_HEADS)
    def _(h):
        w_copy(h, 0).start()
        w_copy(h, 1).start()

    @pl.loop(0, KEY_VALUE_HEADS)
    def _(h):
        q_copy(h).start()

    ends = []
    total = jnp.int32(0)
    for r in range(docs):
        total = total + lengths[0, r]
        ends.append(total)

    def starts_of(place):
        first = jnp.zeros(place.shape, jnp.int32)
        for r in range(docs):
            first = first + jnp.where(place >= ends[r], lengths[0, r], 0)
        return first

    place = s * tokens + lax.broadcasted_iota(jnp.int32, (tokens, HEAD_SIZE), 0)
    angle = (place - starts_of(place)).astype(jnp.float32) * freq[...]
    lane = lax.broadcasted_iota(jnp.int32, (tokens, HEAD_SIZE), 1)
    cosine[...] = jnp.cos(angle)
    turn = jnp.sin(angle)
    sine[...] = jnp.where(lane < HEAD_SIZE // 2, -turn, turn)

    row = s * tokens + lax.broadcasted_iota(jnp.int32, (tokens, tokens), 0)
    first = starts_of(row)
    for d in range(blocks):
        other = (s - d) * tokens + lax.broadcasted_iota(jnp.int32, (tokens, tokens), 1)
        bias[:, d * tokens : (d + 1) * tokens] = jnp.where(
            (other >= first) & (other <= row), 0.0, MASKED
        )

    which = lax.broadcasted_iota(jnp.int32, (docs, tokens), 0)
    token = s * tokens + lax.broadcasted_iota(jnp.int32, (docs, tokens), 1)
    inside = jnp.zeros((docs, tokens), jnp.float32)
    for r in range(docs):
        answer = jnp.minimum(wanted[0, r], lengths[0, r])
        taken = (which == r) & (token < ends[r]) & (token >= ends[r] - answer)
        inside = jnp.where(taken, 1.0, inside)
    member[...] = inside.astype(jnp.bfloat16)
    which = lax.broadcasted_iota(jnp.int32, (docs, pool_width), 0)
    counted = jnp.ones((docs, pool_width), jnp.int32)
    for r in range(docs):
        counted = jnp.where(which == r, jnp.minimum(wanted[0, r], lengths[0, r]), counted)
    answers[...] = counted.astype(jnp.float32)

    for d in range(1, blocks):

        @pl.when(s < d)
        def _():
            kv[d] = jnp.zeros(kv.shape[1:], kv.dtype)

    own_x.wait()
    for k in range(1, n):
        hid_arrival(k).wait_recv()

    @pl.loop(0, KEY_VALUE_HEADS)
    def _(h):
        w_copy(h, 0).wait()
        w_copy(h, 1).wait()
        product[...] = jnp.dot(
            x[...].reshape(n * tokens, depth), w[h], preferred_element_type=jnp.float32
        ).reshape(n, tokens, 2 * HEAD_SIZE)
        outbox[h] = product[...].astype(jnp.bfloat16)
        own[h] = product[f]
        for k in range(1, n):
            sum_copy(h, k).start()

    def finish(h):
        rows = own[h]
        for k in range(1, n):
            sum_arrival(h, k).wait_recv()
            rows = rows + inbox[h, lax.rem(f + k, n)].astype(jnp.float32)
        key = rows[:, :HEAD_SIZE]
        turned = key * cosine[...] + pltpu.roll(key, HEAD_SIZE // 2, 1) * sine[...]
        kv[0, h, :, :HEAD_SIZE] = turned.astype(jnp.bfloat16)
        kv[0, h, :, HEAD_SIZE:] = rows[:, HEAD_SIZE:].astype(jnp.bfloat16)

        @pl.when(sends_up(0))
        def _():
            up_copy(h, 0).start()

        @pl.when(shares_even(0))
        def _():
            pair_copy(h, 0, 0).start()

    def relay(h, i):
        @pl.when(s >= 2 * i)
        def _():
            up_copy(h, i - 1).wait_recv()

        if i < hops:

            @pl.when(sends_up(i))
            def _():
                up_copy(h, i).start()

            @pl.when(shares_even(i))
            def _():
                pair_copy(h, 2 * i, i).start()

        @pl.when(shares_odd(i - 1))
        def _():
            pair_copy(h, 2 * i, i - 1).start()

    scale = HEAD_SIZE**-0.5 * math.log2(math.e)

    def attend(h):
        for m in range(hops):

            @pl.when(s >= 2 * m + 1)
            def _():
                pair_copy(h, 0, m).wait_recv()

        q_copy(h).wait()
        key = kv[:, h, :, :HEAD_SIZE].reshape(blocks * tokens, HEAD_SIZE)
        value = kv[:, h, :, HEAD_SIZE:].reshape(blocks * tokens, HEAD_SIZE)
        for a in range(q_width // HEAD_SIZE):
            lanes = slice(a * HEAD_SIZE, (a + 1) * HEAD_SIZE)
            scores = (
                lax.dot_general(
                    q[h, :, lanes],
                    key,
                    (((1,), (1,)), ((), ())),
                    preferred_element_type=jnp.float32,
                )
                * scale
                + bias[...]
            )
            peak = jnp.max(scores, axis=-1, keepdims=True)
            probs = jnp.exp2(scores - peak)
            norm = jnp.sum(probs, axis=-1, keepdims=True)
            result = jnp.dot(
                probs.astype(jnp.bfloat16), value, preferred_element_type=jnp.float32
            )
            o[h, :, lanes] = (result / norm).astype(jnp.bfloat16)
        o_copy(h).start()
        sums = jnp.dot(member[...], o[h], preferred_element_type=jnp.float32)
        for m in range(per_head):
            j = h * per_head + m
            part[j] = sums[:, m * pool_width : (m + 1) * pool_width]

            @pl.when(j != s)
            def _():
                pool_copy(j).start()

            @pl.when(j == s)
            def _():
                parts[s] = sums[:, m * pool_width : (m + 1) * pool_width]

    @pl.loop(0, KEY_VALUE_HEADS + hops + 1)
    def _(step):
        @pl.when(step < KEY_VALUE_HEADS)
        def _():
            finish(step)

        for i in range(1, hops + 1):

            @pl.when((step >= i) & (step < KEY_VALUE_HEADS + i))
            def _():
                relay(step - i, i)

        @pl.when(step >= hops + 1)
        def _():
            attend(step - hops - 1)

    @pl.loop(1, ranks)
    def _(k):
        pool_arrival(lax.rem(s + k, ranks)).wait_recv()

    sums = parts[0]
    for i in range(1, ranks):
        sums = sums + parts[i]
    pooled[0] = sums / answers[...]

    for k in range(1, n):
        hid_copy(k).wait_send()

    @pl.loop(0, KEY_VALUE_HEADS)
    def _(h):
        for k in range(1, n):
            sum_copy(h, k).wait_send()
        for i in range(hops):

            @pl.when(sends_up(i))
            def _():
                up_copy(h, i).wait_send()

        for m in range(hops):

            @pl.when(shares_even(m))
            def _():
                pair_copy(h, 2 * m, m).wait_send()

            @pl.when(shares_odd(m))
            def _():
                pair_copy(h, 2 * m + 2, m).wait_send()

        o_copy(h).wait()

    @pl.loop(1, ranks)
    def _(k):
        pool_copy(lax.rem(s + k, ranks)).wait_send()


def on_device(hidden, queries, key_value_weight, doc_lengths, resp_lengths):
    n = lax.axis_size("fsdp")
    ranks = lax.axis_size("seq")
    tokens = hidden.shape[1]
    width = hidden.shape[2]
    depth, kv_cols = key_value_weight.shape
    docs = doc_lengths.shape[1]
    q_cols = queries.shape[2]
    q_width = q_cols // KEY_VALUE_HEADS
    pool_width = q_cols // ranks
    hops = ranks // 4
    blocks = 2 * hops + 1
    heads = KEY_VALUE_HEADS
    if depth % HEAD_SIZE:
        hidden = hidden.reshape(tokens, n, depth).transpose(1, 0, 2)
    power = np.arange(HEAD_SIZE // 2, dtype=np.float64) * 2.0 / HEAD_SIZE
    freq = np.tile(ROPE_BASE**-power, 2).astype(np.float32)[None]
    any_space = pl.BlockSpec(memory_space=pl.ANY)
    smem = pl.BlockSpec(memory_space=pltpu.SMEM)
    vmem = pl.BlockSpec(memory_space=pltpu.VMEM)
    dma = pltpu.SemaphoreType.DMA
    bf16, f32 = jnp.bfloat16, jnp.float32
    return pl.pallas_call(
        functools.partial(kernel, n, ranks, hops),
        out_shape=(
            jax.ShapeDtypeStruct((1, tokens, q_cols), bf16),
            jax.ShapeDtypeStruct((1, docs, pool_width), f32),
        ),
        in_specs=[any_space, any_space, any_space, smem, smem, vmem],
        out_specs=(any_space, vmem),
        scratch_shapes=[
            pltpu.VMEM((n, tokens, depth), bf16),
            pltpu.VMEM((heads, depth, 2 * HEAD_SIZE), bf16),
            pltpu.VMEM((heads, tokens, q_width), bf16),
            pltpu.VMEM((n, tokens, 2 * HEAD_SIZE), f32),
            pltpu.VMEM((heads, tokens, 2 * HEAD_SIZE), f32),
            pltpu.VMEM((heads, n, tokens, 2 * HEAD_SIZE), bf16),
            pltpu.VMEM((heads, n, tokens, 2 * HEAD_SIZE), bf16),
            pltpu.VMEM((blocks, heads, tokens, 2 * HEAD_SIZE), bf16),
            pltpu.VMEM((heads, tokens, q_width), bf16),
            pltpu.VMEM((tokens, blocks * tokens), f32),
            pltpu.VMEM((tokens, HEAD_SIZE), f32),
            pltpu.VMEM((tokens, HEAD_SIZE), f32),
            pltpu.VMEM((docs, tokens), bf16),
            pltpu.VMEM((docs, pool_width), f32),
            pltpu.VMEM((ranks, docs, pool_width), f32),
            pltpu.VMEM((ranks, docs, pool_width), f32),
            dma,
            dma((heads, 2)),
            dma((heads,)),
            dma((heads,)),
            dma((n,)),
            dma((n,)),
            dma((heads, n)),
            dma((heads, n)),
            dma((heads, hops)),
            dma((heads, hops)),
            dma((heads, hops)),
            dma((heads, hops)),
            dma((ranks,)),
            dma((ranks,)),
        ],
        compiler_params=pltpu.CompilerParams(
            collective_id=0, has_side_effects=True, vmem_limit_bytes=56 * 2**20
        ),
    )(hidden, queries, key_value_weight, doc_lengths, resp_lengths, jnp.asarray(freq))


def solution(mesh):
    in_specs = (
        P("fsdp", "seq", None),
        P("fsdp", "seq", None),
        P("fsdp", None),
        P("fsdp", None),
        P("fsdp", None),
    )
    out_specs = (P("fsdp", "seq", None), P("fsdp", None, "seq"))
    return jax.shard_map(
        on_device, mesh=mesh, in_specs=in_specs, out_specs=out_specs, check_vma=False
    )
```

time: 268 us -> 65.5 us (0.24); the launches traced: 262 us -> 65.1 us
  other arithmetic: 71.8 us -> 0 us
  Pallas kernels: 0 us -> 60.8 us
  waiting for transfers between devices: 51.9 us -> 0 us
  blocking collectives: 48 us -> 0 us
  local copies, waits for them, and re-layouts: 35.4 us -> 3.61 us
  matrix products: 20.1 us -> 0 us
  starting transfers between devices: 19 us -> 0 us
  between operations: 14.3 us -> 0.64 us
    unnamed x5 -> x0, other arithmetic: 62.7 us -> none
    pallas_call x0 -> x1, Pallas kernels: none -> 60.8 us  [on_device(): pl.pallas_call(functools.partial(kernel, n, ranks, hops), out_shape=(jax....]
    all_to_all x2 -> x0, blocking collectives: 48 us -> none  [the longest x1 29 us: on_device(): lax.all_to_all(attn_heads[None], 'seq', split_axis=1, concat_axis=2, tile...]
    reduce_scatter x1 -> x0, waiting for transfers between devices: 26 us -> none  [on_device(): lax.psum_scatter(partial_value.astype(jnp.bfloat16), 'seq', scatter_dimen...]
    unnamed x29 -> x2, local copies, waits for them, and re-layouts: 24.2 us -> 3.61 us
    dot_general x6 -> x0, matrix products: 20.1 us -> none  [the longest x2 8.34 us: attend(): jnp.einsum('kgqs,skd->qkgd', probs, vblock, preferred_element_type=jnp.fl...]
    unnamed x3 -> x0, waiting for transfers between devices: 20.1 us -> none
    all_to_all x3 -> x0, starting transfers between devices: 19 us -> none  [the longest x1 6.95 us: on_device(): lax.all_to_all(queries, 'seq', split_axis=2, concat_axis=1, tiled=True)]
  transfers between devices with their start and end apart: 5 -> 0, of which waited for: 4 -> 0; matrix products, arithmetic and copies ran while one was open for 16% -> 0% of each run, Pallas kernels for 0% -> 0%
where the time goes in v1:
time: 65.5 us; the launch traced here: 65.1 us
  Pallas kernels  60.8 us (93%)
  local copies, waits for them, and re-layouts  3.61 us (6%)
    pallas_call x1, Pallas kernels, on_device(): pl.pallas_call(functools.partial(kernel, n, ranks, hops), out_shape=(jax....  60.8 us
    unnamed x2, local copies, waits for them, and re-layouts  3.61 us

profile of v1, /device:TPU:25, one launch (start us, length us, event | category | flops | bytes accessed | tf_op | source)
XLA Modules:
  0.0 65.1 jit_solution(4600476195705060315)
XLA Ops:
  0.6 60.8 %shard_map.77 = (bf16[1,128,4096]{2,1,0:T(8,128)(2,1)}, f32[1,8,512]{2,1,0:T(8,128)}) custom-call(bf16[1,128,5120]{2,1,0:T(8,128)(2,1)} %hidden.1, bf16[1,128,4096]{2,1,0:T(8,128)(2,1)} %queries.1, bf16[1280,2048]{1,0:T(8,128)(2,1)} %weight.1, s32[1,8]{1,0:T(1,128)} %lengths.1, s32[1,8]{1,0:T(1,128)} %wanted.1, f32[1,128]{1,0:T(1,128)} %constant.2.clone.freq), custom_call_target="tpu_custom_call" | custom-call | tf_op jit(solution)/shard_map/pallas_call | solution.py:441
  61.5 2.3 %copy.10 = bf16[1,128,4096]{2,1,0:T(8,128)(2,1)} copy(bf16[1,128,4096]{2,1,0:T(8,128)(2,1)} %get-tuple-element.4) | data formatting | bytes 2097152
  63.8 1.3 %copy.11 = f32[1,8,512]{2,1,0:T(8,128)} copy(f32[1,8,512]{2,1,0:T(8,128)} %get-tuple-element.5) | data formatting | bytes 32768

commit v2 on v1

--- a/solution.py
+++ b/solution.py
@@ -28,6 +28,7 @@
     freq,
     attended,
     pooled,
+    raw,
     x,
     w,
     q,
@@ -35,6 +36,9 @@
     own,
     outbox,
     inbox,
+    middle,
+    outbox2,
+    inbox2,
     kv,
     o,
     bias,
@@ -52,6 +56,8 @@
     hid_recv,
     sum_send,
     sum_recv,
+    sum2_send,
+    sum2_recv,
     up_send,
     up_recv,
     pair_send,
@@ -64,10 +70,13 @@
     odd = lax.rem(s, 2)
     partner = s + 1 - 2 * odd
     above = lax.rem(s + 2, ranks)
+    side = math.isqrt(n)
+    fx = lax.rem(f, side)
+    fy = lax.div(f, side)
     tokens = x.shape[1]
     depth = x.shape[2]
     half = weight.shape[1] // 2
-    q_width = q.shape[2]
+    q_width = q.shape[1] // KEY_VALUE_HEADS
     docs = lengths.shape[1]
     blocks = kv.shape[0]
     pool_width = part.shape[2]
@@ -77,21 +86,31 @@
         return pl.ds(pl.multiple_of(start, HEAD_SIZE), size)
 
     def features(j):
-        if len(hidden.shape) == 3 and hidden.shape[0] == n and n > 1:
-            return hidden.at[j]
-        return hidden.at[0, :, columns(j * depth, depth)]
-
-    def w_copy(h, side):
-        return pltpu.make_async_copy(
-            weight.at[:, columns(side * half + h * HEAD_SIZE, HEAD_SIZE)],
-            w.at[h, :, pl.ds(side * HEAD_SIZE, HEAD_SIZE)],
-            w_sem.at[h, side],
-        )
-
-    def q_copy(h):
-        return pltpu.make_async_copy(
-            queries.at[0, :, columns(h * q_width, q_width)], q.at[h], q_sem.at[h]
-        )
+        if len(raw.shape) == 3:
+            return raw.at[j]
+        return raw.at[:, columns(j * depth, depth)]
+
+    pieces = x_sem.shape[0]
+
+    def chunk(source, target, sems, i):
+        rows = source.shape[0] // pieces
+        part_rows = pl.ds(i * rows, rows)
+        return pltpu.make_async_copy(source.at[part_rows], target.at[part_rows], sems.at[i])
+
+    def x_copy(i):
+        if len(raw.shape) == 3:
+            rows = tokens // pieces
+            part_rows = pl.ds(i * rows, rows)
+            return pltpu.make_async_copy(
+                hidden.at[:, part_rows], raw.at[:, part_rows], x_sem.at[i]
+            )
+        return chunk(hidden.at[0], raw, x_sem, i)
+
+    def w_copy(i):
+        return chunk(weight, w, w_sem, i)
+
+    def q_copy(i):
+        return chunk(queries.at[0], q, q_sem, i)
 
     def o_copy(h):
         return pltpu.make_async_copy(
@@ -120,25 +139,59 @@
             device_id_type=MESH,
         )
 
+    def place_of(h):
+        p = lax.rem(h, 2)
+        return p * fy + (1 - p) * fx, p * fx + (1 - p) * fy
+
+    def index_of(h, u, v):
+        p = lax.rem(h, 2)
+        return p * (u * side + v) + (1 - p) * (v * side + u)
+
     def sum_copy(h, k):
-        j = lax.rem(f + k, n)
-        return pltpu.make_async_remote_copy(
-            src_ref=outbox.at[h, j],
-            dst_ref=inbox.at[h, f],
+        u, v = place_of(h)
+        to = lax.rem(u + k, side)
+        return pltpu.make_async_remote_copy(
+            src_ref=outbox.at[h, to],
+            dst_ref=inbox.at[h, u],
             send_sem=sum_send.at[h, k],
-            recv_sem=sum_recv.at[h, f],
-            device_id=(j, s),
+            recv_sem=sum_recv.at[h, u],
+            device_id=(index_of(h, to, v), s),
             device_id_type=MESH,
         )
 
     def sum_arrival(h, k):
-        i = lax.rem(f + k, n)
-        return pltpu.make_async_remote_copy(
-            src_ref=outbox.at[h, i],
-            dst_ref=inbox.at[h, i],
+        u, v = place_of(h)
+        come = lax.rem(u + k, side)
+        return pltpu.make_async_remote_copy(
+            src_ref=outbox.at[h, come],
+            dst_ref=inbox.at[h, come],
             send_sem=sum_send.at[h, k],
-            recv_sem=sum_recv.at[h, i],
-            device_id=(i, s),
+            recv_sem=sum_recv.at[h, come],
+            device_id=(index_of(h, come, v), s),
+            device_id_type=MESH,
+        )
+
+    def sum2_copy(h, k):
+        u, v = place_of(h)
+        to = lax.rem(v + k, side)
+        return pltpu.make_async_remote_copy(
+            src_ref=outbox2.at[h, k],
+            dst_ref=inbox2.at[h, v],
+            send_sem=sum2_send.at[h, k],
+            recv_sem=sum2_recv.at[h, v],
+            device_id=(index_of(h, u, to), s),
+            device_id_type=MESH,
+        )
+
+    def sum2_arrival(h, k):
+        u, v = place_of(h)
+        come = lax.rem(v + k, side)
+        return pltpu.make_async_remote_copy(
+            src_ref=outbox2.at[h, k],
+            dst_ref=inbox2.at[h, come],
+            send_sem=sum2_send.at[h, k],
+            recv_sem=sum2_recv.at[h, come],
+            device_id=(index_of(h, u, come), s),
             device_id_type=MESH,
         )
 
@@ -191,8 +244,12 @@
     def shares_odd(m):
         return (odd == 1) & (s >= 2 * m + 2)
 
-    own_x = pltpu.make_async_copy(features(f), x.at[f], x_sem)
-    own_x.start()
+    for i in range(pieces):
+        x_copy(i).start()
+    for i in range(pieces):
+        w_copy(i).start()
+    for i in range(pieces):
+        q_copy(i).start()
 
     barrier = pltpu.get_barrier_semaphore()
     for k in range(1, n):
@@ -203,18 +260,11 @@
         pl.semaphore_signal(
             barrier, inc=1, device_id=(f, lax.rem(s + k, ranks)), device_id_type=MESH
         )
+    for i in range(pieces):
+        x_copy(i).wait()
     pl.semaphore_wait(barrier, n + ranks - 2)
     for k in range(1, n):
         hid_copy(k).start()
-
-    @pl.loop(0, KEY_VALUE_HEADS)
-    def _(h):
-        w_copy(h, 0).start()
-        w_copy(h, 1).start()
-
-    @pl.loop(0, KEY_VALUE_HEADS)
-    def _(h):
-        q_copy(h).start()
 
     ends = []
     total = jnp.int32(0)
@@ -263,27 +313,54 @@
         def _():
             kv[d] = jnp.zeros(kv.shape[1:], kv.dtype)
 
-    own_x.wait()
+    x[f] = features(f)[...]
+    for i in range(pieces):
+        w_copy(i).wait()
+    for i in range(pieces):
+        q_copy(i).wait()
     for k in range(1, n):
         hid_arrival(k).wait_recv()
 
-    @pl.loop(0, KEY_VALUE_HEADS)
-    def _(h):
-        w_copy(h, 0).wait()
-        w_copy(h, 1).wait()
+    def project(h):
+        strips = [
+            w[:, columns(side_of * half + h * HEAD_SIZE, HEAD_SIZE)] for side_of in range(2)
+        ]
         product[...] = jnp.dot(
-            x[...].reshape(n * tokens, depth), w[h], preferred_element_type=jnp.float32
+            x[...].reshape(n * tokens, depth),
+            jnp.concatenate(strips, axis=1),
+            preferred_element_type=jnp.float32,
         ).reshape(n, tokens, 2 * HEAD_SIZE)
-        outbox[h] = product[...].astype(jnp.bfloat16)
-        own[h] = product[f]
-        for k in range(1, n):
+        u, v = place_of(h)
+        for k in range(1, side):
+            to = lax.rem(u + k, side)
+            for l in range(side):
+                outbox[h, to, l] = product[index_of(h, to, l)].astype(jnp.bfloat16)
             sum_copy(h, k).start()
+        for k in range(side):
+            own[h, k] = product[index_of(h, u, lax.rem(v + k, side))]
+
+    def combine(h):
+        u, v = place_of(h)
+        for k in range(1, side):
+            sum_arrival(h, k).wait_recv()
+        for m in list(range(1, side)) + [0]:
+            rows = own[h, m]
+            for k in range(1, side):
+                rows = rows + inbox[h, lax.rem(u + k, side), lax.rem(v + m, side)].astype(
+                    jnp.float32
+                )
+            if m:
+                outbox2[h, m] = rows.astype(jnp.bfloat16)
+                sum2_copy(h, m).start()
+            else:
+                middle[h] = rows
 
     def finish(h):
-        rows = own[h]
-        for k in range(1, n):
-            sum_arrival(h, k).wait_recv()
-            rows = rows + inbox[h, lax.rem(f + k, n)].astype(jnp.float32)
+        u, v = place_of(h)
+        rows = middle[h]
+        for k in range(1, side):
+            sum2_arrival(h, k).wait_recv()
+            rows = rows + inbox2[h, lax.rem(v + k, side)].astype(jnp.float32)
         key = rows[:, :HEAD_SIZE]
         turned = key * cosine[...] + pltpu.roll(key, HEAD_SIZE // 2, 1) * sine[...]
         kv[0, h, :, :HEAD_SIZE] = turned.astype(jnp.bfloat16)
@@ -325,28 +402,28 @@
             def _():
                 pair_copy(h, 0, m).wait_recv()
 
-        q_copy(h).wait()
         key = kv[:, h, :, :HEAD_SIZE].reshape(blocks * tokens, HEAD_SIZE)
         value = kv[:, h, :, HEAD_SIZE:].reshape(blocks * tokens, HEAD_SIZE)
-        for a in range(q_width // HEAD_SIZE):
-            lanes = slice(a * HEAD_SIZE, (a + 1) * HEAD_SIZE)
-            scores = (
-                lax.dot_general(
-                    q[h, :, lanes],
-                    key,
-                    (((1,), (1,)), ((), ())),
-                    preferred_element_type=jnp.float32,
-                )
-                * scale
-                + bias[...]
-            )
-            peak = jnp.max(scores, axis=-1, keepdims=True)
-            probs = jnp.exp2(scores - peak)
-            norm = jnp.sum(probs, axis=-1, keepdims=True)
-            result = jnp.dot(
-                probs.astype(jnp.bfloat16), value, preferred_element_type=jnp.float32
-            )
-            o[h, :, lanes] = (result / norm).astype(jnp.bfloat16)
+        shared = q_width // HEAD_SIZE
+        query = jnp.concatenate(
+            [q[:, columns(h * q_width + a * HEAD_SIZE, HEAD_SIZE)] for a in range(shared)],
+            axis=0,
+        )
+        scores = lax.dot_general(
+            query, key, (((1,), (1,)), ((), ())), preferred_element_type=jnp.float32
+        ).reshape(shared, tokens, blocks * tokens)
+        scores = scores * scale + bias[...][None]
+        peak = jnp.max(scores, axis=-1, keepdims=True)
+        probs = jnp.exp2(scores - peak)
+        norm = jnp.sum(probs, axis=-1, keepdims=True)
+        result = jnp.dot(
+            probs.astype(jnp.bfloat16).reshape(shared * tokens, blocks * tokens),
+            value,
+            preferred_element_type=jnp.float32,
+        ).reshape(shared, tokens, HEAD_SIZE)
+        result = (result / norm).astype(jnp.bfloat16)
+        for a in range(shared):
+            o[h, :, a * HEAD_SIZE : (a + 1) * HEAD_SIZE] = result[a]
         o_copy(h).start()
         sums = jnp.dot(member[...], o[h], preferred_element_type=jnp.float32)
         for m in range(per_head):
@@ -361,21 +438,17 @@
             def _():
                 parts[s] = sums[:, m * pool_width : (m + 1) * pool_width]
 
-    @pl.loop(0, KEY_VALUE_HEADS + hops + 1)
+    stages = [(0, project), (2, combine), (3, finish)]
+    stages += [(3 + i, functools.partial(relay, i=i)) for i in range(1, hops + 1)]
+    stages += [(4 + hops, attend)]
+
+    @pl.loop(0, KEY_VALUE_HEADS + 4 + hops)
     def _(step):
-        @pl.when(step < KEY_VALUE_HEADS)
-        def _():
-            finish(step)
-
-        for i in range(1, hops + 1):
-
-            @pl.when((step >= i) & (step < KEY_VALUE_HEADS + i))
-            def _():
-                relay(step - i, i)
-
-        @pl.when(step >= hops + 1)
-        def _():
-            attend(step - hops - 1)
+        for lag, stage in stages:
+
+            @pl.when((step >= lag) & (step < KEY_VALUE_HEADS + lag))
+            def _():
+                stage(step - lag)
 
     @pl.loop(1, ranks)
     def _(k):
@@ -391,8 +464,9 @@
 
     @pl.loop(0, KEY_VALUE_HEADS)
     def _(h):
-        for k in range(1, n):
+        for k in range(1, side):
             sum_copy(h, k).wait_send()
+            sum2_copy(h, k).wait_send()
         for i in range(hops):
 
             @pl.when(sends_up(i))
@@ -433,6 +507,9 @@
         hidden = hidden.reshape(tokens, n, depth).transpose(1, 0, 2)
     power = np.arange(HEAD_SIZE // 2, dtype=np.float64) * 2.0 / HEAD_SIZE
     freq = np.tile(ROPE_BASE**-power, 2).astype(np.float32)[None]
+    side = math.isqrt(n)
+    assert side * side == n
+    pieces = 4
     any_space = pl.BlockSpec(memory_space=pl.ANY)
     smem = pl.BlockSpec(memory_space=pltpu.SMEM)
     vmem = pl.BlockSpec(memory_space=pltpu.VMEM)
@@ -447,13 +524,17 @@
         in_specs=[any_space, any_space, any_space, smem, smem, vmem],
         out_specs=(any_space, vmem),
         scratch_shapes=[
+            pltpu.VMEM(hidden.shape[-3 if depth % HEAD_SIZE else -2 :], bf16),
             pltpu.VMEM((n, tokens, depth), bf16),
-            pltpu.VMEM((heads, depth, 2 * HEAD_SIZE), bf16),
-            pltpu.VMEM((heads, tokens, q_width), bf16),
+            pltpu.VMEM((depth, kv_cols), bf16),
+            pltpu.VMEM((tokens, q_cols), bf16),
             pltpu.VMEM((n, tokens, 2 * HEAD_SIZE), f32),
+            pltpu.VMEM((heads, side, tokens, 2 * HEAD_SIZE), f32),
+            pltpu.VMEM((heads, side, side, tokens, 2 * HEAD_SIZE), bf16),
+            pltpu.VMEM((heads, side, side, tokens, 2 * HEAD_SIZE), bf16),
             pltpu.VMEM((heads, tokens, 2 * HEAD_SIZE), f32),
-            pltpu.VMEM((heads, n, tokens, 2 * HEAD_SIZE), bf16),
-            pltpu.VMEM((heads, n, tokens, 2 * HEAD_SIZE), bf16),
+            pltpu.VMEM((heads, side, tokens, 2 * HEAD_SIZE), bf16),
+            pltpu.VMEM((heads, side, tokens, 2 * HEAD_SIZE), bf16),
             pltpu.VMEM((blocks, heads, tokens, 2 * HEAD_SIZE), bf16),
             pltpu.VMEM((heads, tokens, q_width), bf16),
             pltpu.VMEM((tokens, blocks * tokens), f32),
@@ -463,14 +544,16 @@
             pltpu.VMEM((docs, pool_width), f32),
             pltpu.VMEM((ranks, docs, pool_width), f32),
             pltpu.VMEM((ranks, docs, pool_width), f32),
-            dma,
-            dma((heads, 2)),
-            dma((heads,)),
+            dma((pieces,)),
+            dma((pieces,)),
+            dma((pieces,)),
             dma((heads,)),
             dma((n,)),
             dma((n,)),
-            dma((heads, n)),
-            dma((heads, n)),
+            dma((heads, side)),
+            dma((heads, side)),
+            dma((heads, side)),
+            dma((heads, side)),
             dma((heads, hops)),
             dma((heads, hops)),
             dma((heads, hops)),

time: 65.5 us -> 67 us (1.023)
  Pallas kernels: 60.8 us -> 62.5 us
    pallas_call x1, Pallas kernels: 60.8 us -> 62.5 us  [on_device(): pl.pallas_call(functools.partial(kernel, n, ranks, hops), out_shape=(jax....]
where the time goes in v2:
time: 67 us; the launch traced here: 66.7 us
  Pallas kernels  62.5 us (93%)
  local copies, waits for them, and re-layouts  3.61 us (5%)
    pallas_call x1, Pallas kernels, on_device(): pl.pallas_call(functools.partial(kernel, n, ranks, hops), out_shape=(jax....  62.5 us
    unnamed x2, local copies, waits for them, and re-layouts  3.61 us

profile of v2, /device:TPU:25, one launch (start us, length us, event | category | flops | bytes accessed | tf_op | source)
XLA Modules:
  0.0 66.7 jit_solution(4312898314422846978)
XLA Ops:
  0.6 62.5 %shard_map.77 = (bf16[1,128,4096]{2,1,0:T(8,128)(2,1)}, f32[1,8,512]{2,1,0:T(8,128)}) custom-call(bf16[1,128,5120]{2,1,0:T(8,128)(2,1)} %hidden.1, bf16[1,128,4096]{2,1,0:T(8,128)(2,1)} %queries.1, bf16[1280,2048]{1,0:T(8,128)(2,1)} %weight.1, s32[1,8]{1,0:T(1,128)} %lengths.1, s32[1,8]{1,0:T(1,128)} %wanted.1, f32[1,128]{1,0:T(1,128)} %constant.2.clone.freq), custom_call_target="tpu_custom_call" | custom-call | tf_op jit(solution)/shard_map/pallas_call | solution.py:518
  63.1 2.3 %copy.10 = bf16[1,128,4096]{2,1,0:T(8,128)(2,1)} copy(bf16[1,128,4096]{2,1,0:T(8,128)(2,1)} %get-tuple-element.4) | data formatting | bytes 2097152
  65.4 1.3 %copy.11 = f32[1,8,512]{2,1,0:T(8,128)} copy(f32[1,8,512]{2,1,0:T(8,128)} %get-tuple-element.5) | data formatting | bytes 32768

commit v3 on v2

--- a/solution.py
+++ b/solution.py
@@ -28,7 +28,6 @@
     freq,
     attended,
     pooled,
-    raw,
     x,
     w,
     q,
@@ -73,8 +72,11 @@
     side = math.isqrt(n)
     fx = lax.rem(f, side)
     fy = lax.div(f, side)
-    tokens = x.shape[1]
-    depth = x.shape[2]
+    halves = x.shape[0]
+    span = x.shape[2]
+    tokens = halves * span
+    depth = x.shape[3]
+    units = halves * KEY_VALUE_HEADS
     half = weight.shape[1] // 2
     q_width = q.shape[1] // KEY_VALUE_HEADS
     docs = lengths.shape[1]
@@ -85,27 +87,25 @@
     def columns(start, size):
         return pl.ds(pl.multiple_of(start, HEAD_SIZE), size)
 
-    def features(j):
-        if len(raw.shape) == 3:
-            return raw.at[j]
-        return raw.at[:, columns(j * depth, depth)]
-
-    pieces = x_sem.shape[0]
+    def half_head(e):
+        return lax.div(e, KEY_VALUE_HEADS), lax.rem(e, KEY_VALUE_HEADS)
+
+    def features(c, j):
+        rows = pl.ds(pl.multiple_of(c * span, span), span)
+        if depth % HEAD_SIZE:
+            return hidden.at[j, rows]
+        return hidden.at[0, rows, columns(j * depth, depth)]
+
+    pieces = w_sem.shape[0]
+
+    def x_copy(c):
+        return pltpu.make_async_copy(features(c, f), x.at[c, f], x_sem.at[c])
 
     def chunk(source, target, sems, i):
         rows = source.shape[0] // pieces
         part_rows = pl.ds(i * rows, rows)
         return pltpu.make_async_copy(source.at[part_rows], target.at[part_rows], sems.at[i])
 
-    def x_copy(i):
-        if len(raw.shape) == 3:
-            rows = tokens // pieces
-            part_rows = pl.ds(i * rows, rows)
-            return pltpu.make_async_copy(
-                hidden.at[:, part_rows], raw.at[:, part_rows], x_sem.at[i]
-            )
-        return chunk(hidden.at[0], raw, x_sem, i)
-
     def w_copy(i):
         return chunk(weight, w, w_sem, i)
 
@@ -117,24 +117,24 @@
             o.at[h], attended.at[0, :, columns(h * q_width, q_width)], o_sem.at[h]
         )
 
-    def hid_copy(k):
+    def hid_copy(c, k):
         j = lax.rem(f + k, n)
         return pltpu.make_async_remote_copy(
-            src_ref=features(j),
-            dst_ref=x.at[f],
-            send_sem=hid_send.at[k],
-            recv_sem=hid_recv.at[f],
+            src_ref=features(c, j),
+            dst_ref=x.at[c, f],
+            send_sem=hid_send.at[c, k],
+            recv_sem=hid_recv.at[c, f],
             device_id=(j, s),
             device_id_type=MESH,
         )
 
-    def hid_arrival(k):
+    def hid_arrival(c, k):
         i = lax.rem(f + k, n)
         return pltpu.make_async_remote_copy(
-            src_ref=x.at[i],
-            dst_ref=x.at[i],
-            send_sem=hid_send.at[k],
-            recv_sem=hid_recv.at[i],
+            src_ref=x.at[c, i],
+            dst_ref=x.at[c, i],
+            send_sem=hid_send.at[c, k],
+            recv_sem=hid_recv.at[c, i],
             device_id=(i, s),
             device_id_type=MESH,
         )
@@ -195,22 +195,24 @@
             device_id_type=MESH,
         )
 
-    def up_copy(h, i):
-        return pltpu.make_async_remote_copy(
-            src_ref=kv.at[2 * i, h],
-            dst_ref=kv.at[2 * i + 2, h],
-            send_sem=up_send.at[h, i],
-            recv_sem=up_recv.at[h, i],
+    def up_copy(e, i):
+        c, h = half_head(e)
+        return pltpu.make_async_remote_copy(
+            src_ref=kv.at[2 * i, h, c],
+            dst_ref=kv.at[2 * i + 2, h, c],
+            send_sem=up_send.at[e, i],
+            recv_sem=up_recv.at[e, i],
             device_id=(f, above),
             device_id_type=MESH,
         )
 
-    def pair_copy(h, source, m):
-        return pltpu.make_async_remote_copy(
-            src_ref=kv.at[source, h],
-            dst_ref=kv.at[2 * m + 1, h],
-            send_sem=pair_send.at[h, m],
-            recv_sem=pair_recv.at[h, m],
+    def pair_copy(e, source, m):
+        c, h = half_head(e)
+        return pltpu.make_async_remote_copy(
+            src_ref=kv.at[source, h, c],
+            dst_ref=kv.at[2 * m + 1, h, c],
+            send_sem=pair_send.at[e, m],
+            recv_sem=pair_recv.at[e, m],
             device_id=(f, partner),
             device_id_type=MESH,
         )
@@ -244,27 +246,25 @@
     def shares_odd(m):
         return (odd == 1) & (s >= 2 * m + 2)
 
-    for i in range(pieces):
-        x_copy(i).start()
+
+    barrier = pltpu.get_barrier_semaphore()
+    for k in range(1, n):
+        pl.semaphore_signal(
+            barrier, inc=1, device_id=(lax.rem(f + k, n), s), device_id_type=MESH
+        )
+    for k in range(1, ranks):
+        pl.semaphore_signal(
+            barrier, inc=1, device_id=(f, lax.rem(s + k, ranks)), device_id_type=MESH
+        )
+    pl.semaphore_wait(barrier, n + ranks - 2)
+    for k in range(1, n):
+        hid_copy(0, k).start()
+    for c in range(halves):
+        x_copy(c).start()
     for i in range(pieces):
         w_copy(i).start()
     for i in range(pieces):
         q_copy(i).start()
-
-    barrier = pltpu.get_barrier_semaphore()
-    for k in range(1, n):
-        pl.semaphore_signal(
-            barrier, inc=1, device_id=(lax.rem(f + k, n), s), device_id_type=MESH
-        )
-    for k in range(1, ranks):
-        pl.semaphore_signal(
-            barrier, inc=1, device_id=(f, lax.rem(s + k, ranks)), device_id_type=MESH
-        )
-    for i in range(pieces):
-        x_copy(i).wait()
-    pl.semaphore_wait(barrier, n + ranks - 2)
-    for k in range(1, n):
-        hid_copy(k).start()
 
     ends = []
     total = jnp.int32(0)
@@ -281,9 +281,9 @@
     place = s * tokens + lax.broadcasted_iota(jnp.int32, (tokens, HEAD_SIZE), 0)
     angle = (place - starts_of(place)).astype(jnp.float32) * freq[...]
     lane = lax.broadcasted_iota(jnp.int32, (tokens, HEAD_SIZE), 1)
-    cosine[...] = jnp.cos(angle)
+    cosine[...] = jnp.cos(angle).reshape(cosine.shape)
     turn = jnp.sin(angle)
-    sine[...] = jnp.where(lane < HEAD_SIZE // 2, -turn, turn)
+    sine[...] = jnp.where(lane < HEAD_SIZE // 2, -turn, turn).reshape(sine.shape)
 
     row = s * tokens + lax.broadcasted_iota(jnp.int32, (tokens, tokens), 0)
     first = starts_of(row)
@@ -313,97 +313,110 @@
         def _():
             kv[d] = jnp.zeros(kv.shape[1:], kv.dtype)
 
-    x[f] = features(f)[...]
+    for c in range(halves):
+        x_copy(c).wait()
     for i in range(pieces):
         w_copy(i).wait()
     for i in range(pieces):
         q_copy(i).wait()
-    for k in range(1, n):
-        hid_arrival(k).wait_recv()
-
-    def project(h):
+    def project(e):
+        c, h = half_head(e)
+
+        @pl.when(h == 0)
+        def _():
+            for k in range(1, n):
+                hid_arrival(c, k).wait_recv()
+
+            @pl.when(c + 1 < halves)
+            def _():
+                for k in range(1, n):
+                    hid_copy(c + 1, k).start()
+
         strips = [
             w[:, columns(side_of * half + h * HEAD_SIZE, HEAD_SIZE)] for side_of in range(2)
         ]
         product[...] = jnp.dot(
-            x[...].reshape(n * tokens, depth),
+            x[c].reshape(n * span, depth),
             jnp.concatenate(strips, axis=1),
             preferred_element_type=jnp.float32,
-        ).reshape(n, tokens, 2 * HEAD_SIZE)
-        u, v = place_of(h)
+        ).reshape(n, span, 2 * HEAD_SIZE)
+        u, v = place_of(e)
         for k in range(1, side):
             to = lax.rem(u + k, side)
             for l in range(side):
-                outbox[h, to, l] = product[index_of(h, to, l)].astype(jnp.bfloat16)
-            sum_copy(h, k).start()
+                outbox[e, to, l] = product[index_of(e, to, l)].astype(jnp.bfloat16)
+            sum_copy(e, k).start()
         for k in range(side):
-            own[h, k] = product[index_of(h, u, lax.rem(v + k, side))]
-
-    def combine(h):
-        u, v = place_of(h)
+            own[e, k] = product[index_of(e, u, lax.rem(v + k, side))]
+
+    def combine(e):
+        u, v = place_of(e)
         for k in range(1, side):
-            sum_arrival(h, k).wait_recv()
+            sum_arrival(e, k).wait_recv()
         for m in list(range(1, side)) + [0]:
-            rows = own[h, m]
+            rows = own[e, m]
             for k in range(1, side):
-                rows = rows + inbox[h, lax.rem(u + k, side), lax.rem(v + m, side)].astype(
+                rows = rows + inbox[e, lax.rem(u + k, side), lax.rem(v + m, side)].astype(
                     jnp.float32
                 )
             if m:
-                outbox2[h, m] = rows.astype(jnp.bfloat16)
-                sum2_copy(h, m).start()
+                outbox2[e, m] = rows.astype(jnp.bfloat16)
+                sum2_copy(e, m).start()
             else:
-                middle[h] = rows
-
-    def finish(h):
-        u, v = place_of(h)
-        rows = middle[h]
+                middle[e] = rows
+
+    def finish(e):
+        c, h = half_head(e)
+        u, v = place_of(e)
+        rows = middle[e]
         for k in range(1, side):
-            sum2_arrival(h, k).wait_recv()
-            rows = rows + inbox2[h, lax.rem(v + k, side)].astype(jnp.float32)
+            sum2_arrival(e, k).wait_recv()
+            rows = rows + inbox2[e, lax.rem(v + k, side)].astype(jnp.float32)
         key = rows[:, :HEAD_SIZE]
-        turned = key * cosine[...] + pltpu.roll(key, HEAD_SIZE // 2, 1) * sine[...]
-        kv[0, h, :, :HEAD_SIZE] = turned.astype(jnp.bfloat16)
-        kv[0, h, :, HEAD_SIZE:] = rows[:, HEAD_SIZE:].astype(jnp.bfloat16)
+        turned = key * cosine[c] + pltpu.roll(key, HEAD_SIZE // 2, 1) * sine[c]
+        kv[0, h, c, :, :HEAD_SIZE] = turned.astype(jnp.bfloat16)
+        kv[0, h, c, :, HEAD_SIZE:] = rows[:, HEAD_SIZE:].astype(jnp.bfloat16)
 
         @pl.when(sends_up(0))
         def _():
-            up_copy(h, 0).start()
+            up_copy(e, 0).start()
 
         @pl.when(shares_even(0))
         def _():
-            pair_copy(h, 0, 0).start()
-
-    def relay(h, i):
+            pair_copy(e, 0, 0).start()
+
+    def relay(e, i):
         @pl.when(s >= 2 * i)
         def _():
-            up_copy(h, i - 1).wait_recv()
+            up_copy(e, i - 1).wait_recv()
 
         if i < hops:
 
             @pl.when(sends_up(i))
             def _():
-                up_copy(h, i).start()
+                up_copy(e, i).start()
 
             @pl.when(shares_even(i))
             def _():
-                pair_copy(h, 2 * i, i).start()
+                pair_copy(e, 2 * i, i).start()
 
         @pl.when(shares_odd(i - 1))
         def _():
-            pair_copy(h, 2 * i, i - 1).start()
+            pair_copy(e, 2 * i, i - 1).start()
 
     scale = HEAD_SIZE**-0.5 * math.log2(math.e)
 
-    def attend(h):
+    def attend(e):
+        h = lax.rem(e, KEY_VALUE_HEADS)
         for m in range(hops):
 
             @pl.when(s >= 2 * m + 1)
             def _():
-                pair_copy(h, 0, m).wait_recv()
-
-        key = kv[:, h, :, :HEAD_SIZE].reshape(blocks * tokens, HEAD_SIZE)
-        value = kv[:, h, :, HEAD_SIZE:].reshape(blocks * tokens, HEAD_SIZE)
+                for c in range(halves):
+                    pair_copy(c * KEY_VALUE_HEADS + h, 0, m).wait_recv()
+
+        key = kv[:, h, :, :, :HEAD_SIZE].reshape(blocks * tokens, HEAD_SIZE)
+        value = kv[:, h, :, :, HEAD_SIZE:].reshape(blocks * tokens, HEAD_SIZE)
         shared = q_width // HEAD_SIZE
         query = jnp.concatenate(
             [q[:, columns(h * q_width + a * HEAD_SIZE, HEAD_SIZE)] for a in range(shared)],
@@ -438,17 +451,42 @@
             def _():
                 parts[s] = sums[:, m * pool_width : (m + 1) * pool_width]
 
-    stages = [(0, project), (2, combine), (3, finish)]
-    stages += [(3 + i, functools.partial(relay, i=i)) for i in range(1, hops + 1)]
-    stages += [(4 + hops, attend)]
-
-    @pl.loop(0, KEY_VALUE_HEADS + 4 + hops)
+    stages = [(0, 0, project), (2, 0, combine), (3, 0, finish)]
+    stages += [(3 + i, 0, functools.partial(relay, i=i)) for i in range(1, hops + 1)]
+    stages += [(4 + hops, units - KEY_VALUE_HEADS, attend)]
+
+    @pl.loop(0, units + 4 + hops)
     def _(step):
-        for lag, stage in stages:
-
-            @pl.when((step >= lag) & (step < KEY_VALUE_HEADS + lag))
+        for lag, least, stage in stages:
+
+            @pl.when((step >= lag + least) & (step < units + lag))
             def _():
                 stage(step - lag)
+
+    for c in range(halves):
+        for k in range(1, n):
+            hid_copy(c, k).wait_send()
+
+    @pl.loop(0, units)
+    def _(e):
+        for k in range(1, side):
+            sum_copy(e, k).wait_send()
+            sum2_copy(e, k).wait_send()
+        for i in range(hops):
+
+            @pl.when(sends_up(i))
+            def _():
+                up_copy(e, i).wait_send()
+
+        for m in range(hops):
+
+            @pl.when(shares_even(m))
+            def _():
+                pair_copy(e, 2 * m, m).wait_send()
+
+            @pl.when(shares_odd(m))
+            def _():
+                pair_copy(e, 2 * m + 2, m).wait_send()
 
     @pl.loop(1, ranks)
     def _(k):
@@ -459,35 +497,35 @@
         sums = sums + parts[i]
     pooled[0] = sums / answers[...]
 
-    for k in range(1, n):
-        hid_copy(k).wait_send()
-
     @pl.loop(0, KEY_VALUE_HEADS)
     def _(h):
-        for k in range(1, side):
-            sum_copy(h, k).wait_send()
-            sum2_copy(h, k).wait_send()
-        for i in range(hops):
-
-            @pl.when(sends_up(i))
-            def _():
-                up_copy(h, i).wait_send()
-
-        for m in range(hops):
-
-            @pl.when(shares_even(m))
-            def _():
-                pair_copy(h, 2 * m, m).wait_send()
-
-            @pl.when(shares_odd(m))
-            def _():
-                pair_copy(h, 2 * m + 2, m).wait_send()
-
         o_copy(h).wait()
 
     @pl.loop(1, ranks)
     def _(k):
         pool_copy(lax.rem(s + k, ranks)).wait_send()
+
+
+def hand_over(attended, pooled, attended_out, pooled_out, held, held_pooled, sems):
+    pieces = sems.shape[0] - 1
+    rows = attended.shape[1] // pieces
+    chunks = [pl.ds(i * rows, rows) for i in range(pieces)]
+    here = [attended.at[:, c] for c in chunks] + [pooled]
+    kept = [held.at[:, c] for c in chunks] + [held_pooled]
+    there = [attended_out.at[:, c] for c in chunks] + [pooled_out]
+    arrive = [
+        pltpu.make_async_copy(here[i], kept[i], sems.at[i, 0]) for i in range(pieces + 1)
+    ]
+    leave = [
+        pltpu.make_async_copy(kept[i], there[i], sems.at[i, 1]) for i in range(pieces + 1)
+    ]
+    for i in range(pieces + 1):
+        arrive[i].start()
+    for i in range(pieces + 1):
+        arrive[i].wait()
+        leave[i].start()
+    for i in range(pieces + 1):
+        leave[i].wait()
 
 
 def on_device(hidden, queries, key_value_weight, doc_lengths, resp_lengths):
@@ -510,12 +548,16 @@
     side = math.isqrt(n)
     assert side * side == n
     pieces = 4
+    halves = 1
+    span = tokens // halves
+    units = halves * heads
+    pair = 2 * HEAD_SIZE
     any_space = pl.BlockSpec(memory_space=pl.ANY)
     smem = pl.BlockSpec(memory_space=pltpu.SMEM)
     vmem = pl.BlockSpec(memory_space=pltpu.VMEM)
     dma = pltpu.SemaphoreType.DMA
     bf16, f32 = jnp.bfloat16, jnp.float32
-    return pl.pallas_call(
+    results = pl.pallas_call(
         functools.partial(kernel, n, ranks, hops),
         out_shape=(
             jax.ShapeDtypeStruct((1, tokens, q_cols), bf16),
@@ -524,40 +566,39 @@
         in_specs=[any_space, any_space, any_space, smem, smem, vmem],
         out_specs=(any_space, vmem),
         scratch_shapes=[
-            pltpu.VMEM(hidden.shape[-3 if depth % HEAD_SIZE else -2 :], bf16),
-            pltpu.VMEM((n, tokens, depth), bf16),
+            pltpu.VMEM((halves, n, span, depth), bf16),
             pltpu.VMEM((depth, kv_cols), bf16),
             pltpu.VMEM((tokens, q_cols), bf16),
-            pltpu.VMEM((n, tokens, 2 * HEAD_SIZE), f32),
-            pltpu.VMEM((heads, side, tokens, 2 * HEAD_SIZE), f32),
-            pltpu.VMEM((heads, side, side, tokens, 2 * HEAD_SIZE), bf16),
-            pltpu.VMEM((heads, side, side, tokens, 2 * HEAD_SIZE), bf16),
-            pltpu.VMEM((heads, tokens, 2 * HEAD_SIZE), f32),
-            pltpu.VMEM((heads, side, tokens, 2 * HEAD_SIZE), bf16),
-            pltpu.VMEM((heads, side, tokens, 2 * HEAD_SIZE), bf16),
-            pltpu.VMEM((blocks, heads, tokens, 2 * HEAD_SIZE), bf16),
+            pltpu.VMEM((n, span, pair), f32),
+            pltpu.VMEM((units, side, span, pair), f32),
+            pltpu.VMEM((units, side, side, span, pair), bf16),
+            pltpu.VMEM((units, side, side, span, pair), bf16),
+            pltpu.VMEM((units, span, pair), f32),
+            pltpu.VMEM((units, side, span, pair), bf16),
+            pltpu.VMEM((units, side, span, pair), bf16),
+            pltpu.VMEM((blocks, heads, halves, span, pair), bf16),
             pltpu.VMEM((heads, tokens, q_width), bf16),
             pltpu.VMEM((tokens, blocks * tokens), f32),
-            pltpu.VMEM((tokens, HEAD_SIZE), f32),
-            pltpu.VMEM((tokens, HEAD_SIZE), f32),
+            pltpu.VMEM((halves, span, HEAD_SIZE), f32),
+            pltpu.VMEM((halves, span, HEAD_SIZE), f32),
             pltpu.VMEM((docs, tokens), bf16),
             pltpu.VMEM((docs, pool_width), f32),
             pltpu.VMEM((ranks, docs, pool_width), f32),
             pltpu.VMEM((ranks, docs, pool_width), f32),
-            dma((pieces,)),
+            dma((halves,)),
             dma((pieces,)),
             dma((pieces,)),
             dma((heads,)),
-            dma((n,)),
-            dma((n,)),
-            dma((heads, side)),
-            dma((heads, side)),
-            dma((heads, side)),
-            dma((heads, side)),
-            dma((heads, hops)),
-            dma((heads, hops)),
-            dma((heads, hops)),
-            dma((heads, hops)),
+            dma((halves, n)),
+            dma((halves, n)),
+            dma((units, side)),
+            dma((units, side)),
+            dma((units, side)),
+            dma((units, side)),
+            dma((units, hops)),
+            dma((units, hops)),
+            dma((units, hops)),
+            dma((units, hops)),
             dma((ranks,)),
             dma((ranks,)),
         ],
@@ -565,6 +606,13 @@
             collective_id=0, has_side_effects=True, vmem_limit_bytes=56 * 2**20
         ),
     )(hidden, queries, key_value_weight, doc_lengths, resp_lengths, jnp.asarray(freq))
+    return pl.pallas_call(
+        hand_over,
+        out_shape=tuple(jax.ShapeDtypeStruct(r.shape, r.dtype) for r in results),
+        in_specs=[any_space, any_space],
+        out_specs=(any_space, any_space),
+        scratch_shapes=[pltpu.VMEM(r.shape, r.dtype) for r in results] + [dma((pieces + 1, 2))],
+    )(*results)
 
 
 def solution(mesh):

time: 67 us -> 65.4 us (0.976)
  local copies, waits for them, and re-layouts: 3.61 us -> 0 us
  Pallas kernels: 62.5 us -> 64.5 us
    unnamed x2 -> x0, local copies, waits for them, and re-layouts: 3.61 us -> none
    pallas_call x0 -> x1, Pallas kernels: none -> 2 us  [on_device(): pl.pallas_call(hand_over, out_shape=tuple((jax.ShapeDtypeStruct(r.shape,...]
where the time goes in v3:
time: 65.4 us; the launch traced here: 65.2 us
  Pallas kernels  64.5 us (99%)
    pallas_call x1, Pallas kernels, on_device(): pl.pallas_call(functools.partial(kernel, n, ranks, hops), out_shape=(jax....  62.5 us
    pallas_call x1, Pallas kernels, on_device(): pl.pallas_call(hand_over, out_shape=tuple((jax.ShapeDtypeStruct(r.shape,...  2 us

profile of v3, /device:TPU:25, one launch (start us, length us, event | category | flops | bytes accessed | tf_op | source)
XLA Modules:
  0.0 65.2 jit_solution(2509028443117278377)
XLA Ops:
  0.6 62.5 %shard_map.77 = (bf16[1,128,4096]{2,1,0:T(8,128)(2,1)}, f32[1,8,512]{2,1,0:T(8,128)}) custom-call(bf16[1,128,5120]{2,1,0:T(8,128)(2,1)} %hidden.1, bf16[1,128,4096]{2,1,0:T(8,128)(2,1)} %queries.1, bf16[1280,2048]{1,0:T(8,128)(2,1)} %weight.1, s32[1,8]{1,0:T(1,128)} %lengths.1, s32[1,8]{1,0:T(1,128)} %wanted.1, f32[1,128]{1,0:T(1,128)} %constant.2.clone.freq), custom_call_target="tpu_custom_call" | custom-call | tf_op jit(solution)/shard_map/pallas_call | solution.py:560
  63.2 2.0 %shard_map.78 = (bf16[1,128,4096]{2,1,0:T(8,128)(2,1)}, f32[1,8,512]{2,1,0:T(8,128)}) custom-call(bf16[1,128,4096]{2,1,0:T(8,128)(2,1)} %get-tuple-element.4.attended, f32[1,8,512]{2,1,0:T(8,128)} %get-tuple-element.5.pooled), custom_call_target="tpu_custom_call" | custom-call | tf_op jit(solution)/shard_map/pallas_call | solution.py:609
